TPU v7x, 256 devices: a whole 4x4x8 slice. The times are simulated.
256 devices in a mesh: row: 32 (over z, x), col: 8 (over y, core).
Axes of the slice: x: 4, y: 4, z: 8, core: 2. Of those that a mesh axis runs over, the one named last changes fastest.
Arguments:
- modes: float32 [131072, 2048], P('row', 'col'), may hold values from -6 to 6
- panel_one: float32 [131072, 256], P('row', 'col'), may hold values from -0.015625 to 0.015625
- panel_two: float32 [131072, 256], P('row', 'col'), may hold values from -0.015625 to 0.015625
- factor_one: float32 [256, 256], replicated, may hold values from -1 to 2, as said below
- factor_two: float32 [256, 256], replicated, may hold values from -1 to 2, as said below
Outputs:
- updated: float32 [131072, 2048], P('row', 'col')
- coordinates: float32 [512, 2048], P(None, 'col')
Inputs may be any that keep to these rules, and one draw needn't show every extreme that they name: factor_one is upper triangular with diagonal entries between 1 and 2. factor_two is upper triangular with diagonal entries between 1 and 2.
All inputs are finite; a program needn't handle non-finite values.
Results may differ from a plain program's by a relative error of at most 0.000086.
Values sent between devices are 32-bit elements; how exact they have to be, the bound alone decides.
A program may use at most 64 MiB of HBM per device.

v0:
```python
import jax
import jax.numpy as jnp
from jax import lax
from jax.sharding import PartitionSpec as P

precise = lax.Precision.HIGHEST


def contract(left, right):
    return lax.dot_general(
        left, right, (((0,), (0,)), ((), ())), precision=precise, preferred_element_type=jnp.float32
    )


def product(left, right):
    return jnp.dot(left, right, precision=precise, preferred_element_type=jnp.float32)


def apply_panel(vectors, panel, factor):
    gathered = lax.all_gather(panel, "col", axis=1, tiled=True)
    partial_value = contract(gathered, vectors)
    coords = product(factor, lax.psum(partial_value, "row"))
    return (vectors - product(gathered, coords), coords)


def shards(modes, panel_one, panel_two, factor_one, factor_two):
    middle, coord_two = apply_panel(modes, panel_two, factor_two)
    updated, coord_one = apply_panel(middle, panel_one, factor_one)
    return (updated, jnp.concatenate([coord_one, coord_two], axis=0))


def solution(mesh):
    return jax.shard_map(
        shards,
        mesh=mesh,
        in_specs=(P("row", "col"), P("row", "col"), P("row", "col"), P(), P()),
        out_specs=(P("row", "col"), P(None, "col")),
        check_vma=False,
    )
```

profile of v0, /device:TPU:1, one launch (start us, length us, event | category | flops | bytes accessed | tf_op | source)
XLA Modules:
  0.0 404.3 jit_solution(676203170181935238)
XLA Ops:
  7.2 0.0 copy-start
  7.2 0.0 all-gather.3.cloned.1.call-start
  7.2 0.7 all-gather.3.cloned.1.call-update
  7.9 0.0 all-reduce.3.cloned.1.call-start
  8.0 40.9 %all-gather.3.cloned.1.call-done = f32[4096,256]{0,1:T(8,128)} async-done(((f32[4096,32]{0,1:T(8,128)}), f32[4096,256]{0,1:T(8,128)}) %all-gather.3.cloned.1.call-update) | async-done | bytes 4194320 | tf_op jit(solution)/shard_map/all_gather | solution.py:20
  48.8 7.8 %fusion.2 = f32[256,256]{1,0:T(8,128)} fusion(f32[4096,256]{0,1:T(8,128)} %all-gather.3.cloned.1.call-done, f32[4096,256]{1,0:T(8,128)} %param.5), kind=kOutput, calls=%fused_computation.6 | convolution fusion | flops 3221225472 | bytes 8650752 | tf_op jit(solution)/shard_map/dot_general | solution.py:10
  56.6 0.0 all-reduce.3.cloned.1.call-update
  56.6 0.0 all-gather.5.cloned.1.call-start
  56.7 0.7 all-gather.5.cloned.1.call-update
  57.3 0.2 all-reduce.5.cloned.1.call-start
  57.6 5.6 %copy.7 = f32[4096,256]{0,1:T(8,128)} copy(f32[4096,256]{1,0:T(8,128)} %param.5) | data formatting | bytes 8388608 | tf_op args[0]
  63.2 132.6 %all-reduce.3.cloned.1.call-done = f32[256,256]{1,0:T(8,128)} async-done(((f32[256,256]{1,0:T(8,128)}), f32[256,256]{1,0:T(8,128)}) %all-reduce.3.cloned.1.call-update) | async-done | bytes 262160 | tf_op jit(solution)/shard_map/psum | solution.py:22
  195.8 0.0 copy-done
  195.8 1.3 fusion.3
  197.2 8.8 %fusion.1 = f32[4096,256]{0,1:T(8,128)} fusion(f32[4096,256]{0,1:T(8,128)} %copy.7, f32[256,256]{0,1:T(8,128)S(1)} %fusion.3, f32[4096,256]{0,1:T(8,128)} %all-gather.3.cloned.1.call-done), kind=kOutput, calls=%fused_computation.3 | convolution fusion | flops 3222274048 | bytes 12845056 | tf_op jit(solution)/shard_map/dot_general | solution.py:16
  206.0 28.3 %all-gather.5.cloned.1.call-done = f32[4096,256]{0,1:T(8,128)} async-done(((f32[4096,32]{0,1:T(8,128)}), f32[4096,256]{0,1:T(8,128)}) %all-gather.5.cloned.1.call-update) | async-done | bytes 4194320 | tf_op jit(solution)/shard_map/all_gather | solution.py:20
  234.3 7.7 %convolution_bitcast_fusion.2 = f32[256,256]{0,1:T(8,128)} fusion(f32[4096,256]{0,1:T(8,128)} %fusion.1, f32[4096,256]{0,1:T(8,128)} %all-gather.5.cloned.1.call-done), kind=kOutput, calls=%fused_computation.4 | convolution fusion | flops 3221225472 | bytes 8650752 | tf_op jit(solution)/shard_map/dot_general | solution.py:10
  241.9 0.0 all-reduce.5.cloned.1.call-update
  242.0 139.2 %all-reduce.5.cloned.1.call-done = f32[256,256]{0,1:T(8,128)} async-done(((f32[256,256]{0,1:T(8,128)}), f32[256,256]{0,1:T(8,128)}) %all-reduce.5.cloned.1.call-update) | async-done | bytes 262160 | tf_op jit(solution)/shard_map/psum | solution.py:22
  381.1 0.0 copy-done.1
  381.1 1.4 fusion.4
  382.5 8.8 %fusion = f32[4096,256]{0,1:T(8,128)} fusion(f32[4096,256]{0,1:T(8,128)} %fusion.1, f32[256,256]{0,1:T(8,128)S(1)} %fusion.4, f32[4096,256]{0,1:T(8,128)} %all-gather.5.cloned.1.call-done), kind=kOutput, calls=%fused_computation.1 | convolution fusion | flops 3222274048 | bytes 12845056 | tf_op jit(solution)/shard_map/dot_general | solution.py:16
  391.3 5.6 %copy.8 = f32[4096,256]{1,0:T(8,128)} copy(f32[4096,256]{0,1:T(8,128)} %fusion) | data formatting | bytes 8388608
  396.9 0.8 pad_maximum_fusion
  (1 shorter events, 0.0 us)
Async XLA Ops:
  7.2 188.6 %copy-start = (f32[256,256]{1,0:T(8,128)S(1)}, f32[256,256]{1,0:T(8,128)}, u32[]{:S(2)}) copy-start(f32[256,256]{1,0:T(8,128)} %param.9) | copy-start | bytes 786436
  7.2 41.6 %all-gather.3.cloned.1.call-start = ((), (), s32[]{:S(2)}) async-start(), calls=%async_computation | async-start | bytes 4718592 | tf_op jit(solution)/shard_map/all_gather | solution.py:20
  7.9 187.9 %all-reduce.3.cloned.1.call-start = ((), (), s32[]{:S(2)}) async-start(), calls=%async_computation.1 | async-start | bytes 524288 | tf_op jit(solution)/shard_map/psum | solution.py:22
  56.6 177.6 %all-gather.5.cloned.1.call-start = ((), (), s32[]{:S(2)}) async-start(), calls=%async_computation.2 | async-start | bytes 4718592 | tf_op jit(solution)/shard_map/all_gather | solution.py:20
  57.3 323.8 %all-reduce.5.cloned.1.call-start = ((), (), s32[]{:S(2)}) async-start(), calls=%async_computation.3 | async-start | bytes 524288 | tf_op jit(solution)/shard_map/psum | solution.py:22
  206.0 175.2 %copy-start.1 = (f32[256,256]{1,0:T(8,128)S(1)}, f32[256,256]{1,0:T(8,128)}, u32[]{:S(2)}) copy-start(f32[256,256]{1,0:T(8,128)} %param.8) | copy-start | bytes 786436
Sparse Core Ops, SparseCore 0:
  9.9 38.8 all-gather.2
  56.7 139.0 all-reduce.2
  197.7 36.5 all-gather.4
  242.1 139.0 all-reduce.4
where the time goes:
time: 408 us; the launch traced here: 404 us
  waiting for transfers between devices  342 us (84%)
  matrix products  35.8 us (9%)
  between operations  13.8 us (3%)
  local copies, waits for them, and re-layouts  11.2 us (3%)
    psum x2, waiting for transfers between devices, apply_panel(): coords = product(factor, lax.psum(partial_value, 'row'))  272 us
    all_gather x2, waiting for transfers between devices, apply_panel(): gathered = lax.all_gather(panel, 'col', axis=1, tiled=True)  69.2 us
    dot_general x4, matrix products, product(): jnp.dot(left, right, precision=precise, preferred_element_type=jnp.float32)  20.3 us
    dot_general x2, matrix products, contract(): lax.dot_general(left, right, (((0,), (0,)), ((), ())), precision=precise,...  15.5 us
    unnamed x6, local copies, waits for them, and re-layouts  11.2 us
  transfers between devices with their start and end apart: 4, of which 4 were waited for; matrix products, arithmetic and copies ran while one was open for 4% of the time, Pallas kernels for 0%

commit v1 on v0

v1 whole, which is shorter than its diff:
```python
import functools

import jax
import jax.numpy as jnp
from jax import lax
from jax.experimental import pallas as pl
from jax.experimental.pallas import tpu as pltpu
from jax.sharding import PartitionSpec as P

MESH = pl.DeviceIdType.MESH
F32, BF16 = jnp.float32, jnp.bfloat16
ROWS, COLS, NB = 4096, 256, 256
SHARE = 32
UNITS, UNIT = 4, 8
HALF = ROWS // 2
NX, NY, NZ = 4, 4, 8
GRAM = 8
STEP = 1024
PLACE = {0: 0, 1: 1, 3: 2, 2: 3}
AWAY = [0, 1, 3, 2]


def split(value):
    high = value.astype(BF16)
    return high, (value - high.astype(F32)).astype(BF16)


def dot(a, b):
    return jnp.dot(a, b, preferred_element_type=F32)


def exact(a, b):
    return jnp.dot(a, b, precision=lax.Precision.HIGHEST, preferred_element_type=F32)


def kernel(
    modes, panel_one, panel_two, factor_one, factor_two, updated, coords,
    work, gathered, mode_high, mode_low, high, low, factors, part, from_x, from_z, sums, gram, right_side,
    load_sem, own_send, own_recv, fwd_send, fwd_recv, sib_send, sib_recv,
    x_send, x_recv, z_send, z_recv, back_send, back_recv, gram_send, gram_recv, gsib_send, gsib_recv, out_sem,
):
    row, col = lax.axis_index("row"), lax.axis_index("col")
    z, x, y, k = row // NX, row % NX, col // 2, col % 2
    up, down = (row, lax.rem(y + 1, NY) * 2 + k), (row, lax.rem(y + NY - 1, NY) * 2 + k)
    sibling = (row, y * 2 + 1 - k)
    across = (row, lax.rem(y + 2, NY) * 2 + k)
    x_peer = [None] + [(z * NX + lax.rem(x + d, NX), col) for d in range(1, NX)]
    z_peer = [None] + [(lax.rem(z + d, NZ) * NX + x, col) for d in range(1, NZ)]
    panels = (panel_two, panel_one)
    mine = pl.ds(pl.multiple_of(k * SHARE, SHARE), SHARE)
    sends = []

    def remote(src, dst, send, recv, device):
        copy = pltpu.make_async_remote_copy(
            src_ref=src, dst_ref=dst, send_sem=send, recv_sem=recv, device_id=device, device_id_type=MESH
        )
        copy.start()
        sends.append(copy)
        return copy

    loads = []
    for p in range(2):
        loads.append(pltpu.make_async_copy(panels[p], gathered.at[p, mine], load_sem.at[p]))
    for i in range(8):
        rows = pl.ds(i * 512, 512)
        loads.append(pltpu.make_async_copy(modes.at[rows], work.at[rows], load_sem.at[4 + i]))
    loads.append(pltpu.make_async_copy(factor_two, factors.at[0], load_sem.at[2]))
    loads.append(pltpu.make_async_copy(factor_one, factors.at[1], load_sem.at[3]))
    for copy in loads:
        copy.start()

    barrier = pltpu.get_barrier_semaphore()
    friends = [up, down, across, sibling] + x_peer[1:] + z_peer[1:]
    for device in friends:
        pl.semaphore_signal(barrier, inc=1, device_id=device, device_id_type=MESH)
    pl.semaphore_wait(barrier, len(friends))

    def unit_rows(place, u):
        return pl.ds(pl.multiple_of(place * 64 + k * SHARE + u * UNIT, UNIT), UNIT)

    def send_own(p):
        got = {}
        for u in range(UNITS):
            src = panels[p].at[pl.ds(u * UNIT, UNIT)]
            for way, (device, away) in enumerate(((up, 3), (down, 1))):
                got[way, u] = remote(
                    src, gathered.at[p, unit_rows(PLACE[away], u)], own_send.at[p, way, u], own_recv.at[p, way, u], device
                )
        return got

    def to_sibling(p, place, u):
        rows = unit_rows(place, u)
        return remote(
            gathered.at[p, rows], gathered.at[p, rows], sib_send.at[p, place, u], sib_recv.at[p, place, u], sibling
        )

    def pass_on(p, own, u):
        copies = []
        for way, (device, away) in enumerate(((up, 3), (down, 1))):
            own[way, u].wait_recv()
            lanes = pl.ds(way * HALF, HALF)
            copies.append(remote(
                gathered.at[p, unit_rows(PLACE[away], u), lanes], gathered.at[p, unit_rows(3, u), lanes],
                fwd_send.at[p, way, u], fwd_recv.at[p, way, u], device,
            ))
        return copies, [to_sibling(p, PLACE[away], u) for away in (3, 1)]

    def multiply(p, place, group):
        total = jnp.zeros((64, COLS), F32)
        for i in range(ROWS // STEP):
            lanes = slice(i * STEP, (i + 1) * STEP)
            h, l = split(gathered[p, place * 64:(place + 1) * 64, lanes])
            two = dot(jnp.concatenate([h, l], axis=0), mode_high[lanes])
            total += two[:64] + two[64:] + dot(h, mode_low[lanes])
        part[group] = total

    def turn(p, pair):
        for i in range(ROWS // STEP):
            lanes = slice(i * STEP, (i + 1) * STEP)
            h, l = split(gathered[p, pair * 128:(pair + 1) * 128, lanes].T)
            high[p, lanes, pair * 128:(pair + 1) * 128] = h
            low[p, lanes, pair * 128:(pair + 1) * 128] = l

    class Group:
        def __init__(self, group, count, target, base):
            self.group, self.m, self.target, self.base = group, count // NX, target, base

        def piece(self, at):
            return pl.ds(pl.multiple_of(at * self.m, self.m), self.m)

        def share_out(self):
            g, m = self.group, self.m
            self.copies = [
                remote(part.at[g, self.piece(lax.rem(x + d, NX))], from_x.at[g, d - 1, pl.ds(0, m)],
                       x_send.at[g, d - 1], x_recv.at[g, d - 1], x_peer[d])
                for d in range(1, NX)
            ]

        def exchange(self):
            g, m = self.group, self.m
            for copy in self.copies:
                copy.wait_recv()
            from_z[g, z, 0:m] = part[g, self.piece(x)] + from_x[g, 0, 0:m] + from_x[g, 1, 0:m] + from_x[g, 2, 0:m]
            self.copies = [
                remote(from_z.at[g, z, pl.ds(0, m)], from_z.at[g, z, pl.ds(0, m)],
                       z_send.at[g, d - 1], z_recv.at[g, d - 1], z_peer[d])
                for d in range(1, NZ)
            ]

        def collect(self):
            g, m = self.group, self.m
            for copy in self.copies:
                copy.wait_recv()
            total = from_z[g, 0, 0:m]
            for i in range(1, NZ):
                total += from_z[g, i, 0:m]
            rows = pl.ds(pl.multiple_of(self.base + x * m, m), m)
            self.target[rows] = total
            self.copies = [
                remote(self.target.at[rows], self.target.at[rows], back_send.at[g, d - 1], back_recv.at[g, d - 1], x_peer[d])
                for d in range(1, NX)
            ]

        def finish(self):
            for copy in self.copies:
                copy.wait_recv()

    def y_of(place):
        return lax.rem(y + AWAY[place], NY)

    groups = {
        (p, s): Group(p * 4 + s, 64, sums.at[p], pl.multiple_of(y_of(s) * 64, 64)) for p in range(2) for s in range(4)
    }
    gram_group = Group(GRAM, SHARE, gram, pl.multiple_of(k * SHARE, SHARE))

    def local(value, home):
        return jnp.concatenate(
            [value[pl.ds(pl.multiple_of(lax.rem(home + AWAY[s], NY) * 64, 64), 64)] for s in range(4)], axis=0
        )

    own_two = send_own(0)
    sib_own = []
    for p in range(2):
        for u in range(UNITS):
            rows = unit_rows(0, u)
            sib_own.append(remote(
                panels[p].at[pl.ds(u * UNIT, UNIT)], gathered.at[p, rows], sib_send.at[p, 0, u], sib_recv.at[p, 0, u], sibling
            ))
    for copy in loads:
        copy.wait()
    for i in range(8):
        rows = slice(i * 512, (i + 1) * 512)
        mode_high[rows], mode_low[rows] = split(work[rows])
    for copy in sib_own:
        copy.wait_recv()
    for p in range(2):
        multiply(p, 0, p * 4)
        groups[p, 0].share_out()

    passed, siblings = [], []

    def relay(p, own, u):
        a, b = pass_on(p, own, u)
        passed.append(a)
        siblings.extend(b)

    relay(0, own_two, 0)
    for p in range(2):
        groups[p, 0].exchange()
    relay(0, own_two, 1)
    relay(0, own_two, 2)
    for p in range(2):
        groups[p, 0].collect()
    relay(0, own_two, 3)
    own_one = send_own(1)
    for copy in siblings:
        copy.wait_recv()
    passed_two, passed, siblings = passed, [], []
    for s in (1, 2):
        multiply(0, s, s)
        groups[0, s].share_out()
    turn(0, 0)
    last = []
    for u in range(UNITS):
        for copy in passed_two[u]:
            copy.wait_recv()
        last.append(to_sibling(0, 3, u))
    for s in (1, 2):
        groups[0, s].exchange()
    for copy in last:
        copy.wait_recv()
    multiply(0, 3, 3)
    groups[0, 3].share_out()
    turn(0, 1)
    relay(1, own_one, 0)

    total = jnp.zeros((SHARE, NB), F32)
    for i in range(ROWS // STEP):
        lanes = slice(i * STEP, (i + 1) * STEP)
        h, l = split(gathered[1, mine, lanes])
        two = dot(jnp.concatenate([h, l], axis=0), high[0, lanes])
        total += two[:SHARE] + two[SHARE:] + dot(h, low[0, lanes])
    part[GRAM, 0:SHARE] = total
    gram_group.share_out()
    groups[0, 3].exchange()
    for s in (1, 2):
        groups[0, s].collect()
    relay(1, own_one, 1)
    gram_group.exchange()
    groups[0, 3].collect()
    relay(1, own_one, 2)
    gram_group.collect()
    relay(1, own_one, 3)
    for copy in siblings:
        copy.wait_recv()
    for s in (1, 2):
        multiply(1, s, 4 + s)
        groups[1, s].share_out()
    turn(1, 0)
    last = []
    for u in range(UNITS):
        for copy in passed[u]:
            copy.wait_recv()
        last.append(to_sibling(1, 3, u))
    for s in (1, 2):
        groups[1, s].exchange()
    for copy in last:
        copy.wait_recv()
    multiply(1, 3, 7)
    groups[1, 3].share_out()
    turn(1, 1)
    gram_group.finish()
    around = [
        remote(gram.at[mine], gram.at[pl.ds(pl.multiple_of(away * 64 + k * SHARE, SHARE), SHARE)],
               gram_send.at[away], gram_recv.at[away], device)
        for away, device in ((3, up), (1, down), (2, across))
    ]
    for s in range(4):
        groups[0, s].finish()
    coord_two = exact(factors[0], sums[0])
    coords[NB:2 * NB] = coord_two
    groups[1, 3].exchange()
    for s in (1, 2):
        groups[1, s].collect()
    for copy in around:
        copy.wait_recv()
    swap = []
    for away in range(4):
        rows = pl.ds(pl.multiple_of(away * 64 + k * SHARE, SHARE), SHARE)
        swap.append(remote(gram.at[rows], gram.at[rows], gsib_send.at[away], gsib_recv.at[away], sibling))

    def update(p, c, emit):
        ch, cl = split(c)
        for i in range(8):
            rows = slice(i * 512, (i + 1) * 512)
            h = high[p, rows]
            emit(rows, work[rows] - (dot(h, ch) + dot(low[p, rows], ch) + dot(h, cl)))

    def keep(rows, value):
        work[rows] = value

    two_at = coords.at[NB:2 * NB]
    update(0, local(two_at, y), keep)
    for copy in swap:
        copy.wait_recv()
    for away in range(4):
        home = lax.rem(y + away, NY)
        right_side[pl.ds(pl.multiple_of(home * 64, 64), 64)] = exact(gram[away * 64:(away + 1) * 64], local(two_at, home))
    groups[1, 3].collect()
    for s in range(4):
        groups[1, s].finish()
    coords[0:NB] = exact(factors[1], sums[1] - right_side[...])
    outs = []

    def emit(rows, value):
        work[rows] = value
        copy = pltpu.make_async_copy(work.at[rows], updated.at[rows], out_sem.at[rows.start // 512])
        copy.start()
        outs.append(copy)

    update(1, local(coords.at[0:NB], y), emit)
    for copy in sends:
        copy.wait_send()
    for copy in outs:
        copy.wait()


def shards(modes, panel_one, panel_two, factor_one, factor_two):
    hbm = pl.BlockSpec(memory_space=pltpu.HBM)
    dma = pltpu.SemaphoreType.DMA
    return pl.pallas_call(
        kernel,
        out_shape=(jax.ShapeDtypeStruct((ROWS, COLS), F32), jax.ShapeDtypeStruct((2 * NB, COLS), F32)),
        in_specs=[hbm] * 5,
        out_specs=(hbm, pl.BlockSpec(memory_space=pltpu.VMEM)),
        scratch_shapes=[
            pltpu.VMEM((ROWS, COLS), F32),
            pltpu.VMEM((2, NB, ROWS), F32),
            pltpu.VMEM((ROWS, COLS), BF16),
            pltpu.VMEM((ROWS, COLS), BF16),
            pltpu.VMEM((2, ROWS, NB), BF16),
            pltpu.VMEM((2, ROWS, NB), BF16),
            pltpu.VMEM((2, NB, NB), F32),
            pltpu.VMEM((9, 64, COLS), F32),
            pltpu.VMEM((9, NX - 1, 16, COLS), F32),
            pltpu.VMEM((9, NZ, 16, COLS), F32),
            pltpu.VMEM((2, NB, COLS), F32),
            pltpu.VMEM((NB, NB), F32),
            pltpu.VMEM((NB, COLS), F32),
            dma((12,)),
            dma((2, 2, UNITS)), dma((2, 2, UNITS)),
            dma((2, 2, UNITS)), dma((2, 2, UNITS)),
            dma((2, 4, UNITS)), dma((2, 4, UNITS)),
            dma((9, NX - 1)), dma((9, NX - 1)),
            dma((9, NZ - 1)), dma((9, NZ - 1)),
            dma((9, NX - 1)), dma((9, NX - 1)),
            dma((4,)), dma((4,)),
            dma((4,)), dma((4,)),
            dma((8,)),
        ],
        compiler_params=pltpu.CompilerParams(collective_id=0, has_side_effects=True, vmem_limit_bytes=56 << 20),
    )(modes, panel_one.T, panel_two.T, factor_one, factor_two)


def solution(mesh):
    return jax.shard_map(
        shards,
        mesh=mesh,
        in_specs=(P("row", "col"), P("row", "col"), P("row", "col"), P(), P()),
        out_specs=(P("row", "col"), P(None, "col")),
        check_vma=False,
    )
```

time: 408 us -> 81 us (0.20)
  waiting for transfers between devices: 342 us -> 0 us
  Pallas kernels: 0 us -> 74.9 us
  matrix products: 35.8 us -> 0 us
  between operations: 13.8 us -> 0.65 us
  local copies, waits for them, and re-layouts: 11.2 us -> 5.33 us
    psum x2 -> x0, waiting for transfers between devices: 272 us -> none  [apply_panel(): coords = product(factor, lax.psum(partial_value, 'row'))]
    pallas_call x0 -> x1, Pallas kernels: none -> 74.9 us  [shards(): pl.pallas_call(kernel, out_shape=(jax.ShapeDtypeStruct((ROWS, COLS), F32)...]
    all_gather x2 -> x0, waiting for transfers between devices: 69.2 us -> none  [apply_panel(): gathered = lax.all_gather(panel, 'col', axis=1, tiled=True)]
    dot_general x6 -> x0, matrix products: 35.8 us -> none  [the longest x4 20.3 us: product(): jnp.dot(left, right, precision=precise, preferred_element_type=jnp.float32)]
    unnamed x6 -> x4, local copies, waits for them, and re-layouts: 11.2 us -> 5.33 us
  transfers between devices with their start and end apart: 4 -> 0, of which waited for: 4 -> 0; matrix products, arithmetic and copies ran while one was open for 4% -> 0% of each run, Pallas kernels for 0% -> 0%
where the time goes in v1:
time: 81 us; the launch traced here: 80.9 us
  Pallas kernels  74.9 us (92%)
  local copies, waits for them, and re-layouts  5.33 us (7%)
    pallas_call x1, Pallas kernels, shards(): pl.pallas_call(kernel, out_shape=(jax.ShapeDtypeStruct((ROWS, COLS), F32)...  74.9 us
    unnamed x4, local copies, waits for them, and re-layouts  5.33 us

profile of v1, /device:TPU:1, one launch (start us, length us, event | category | flops | bytes accessed | tf_op | source)
XLA Modules:
  0.0 80.9 jit_solution(14406744740924203194)
XLA Ops:
  0.6 74.9 %shard_map.68 = (f32[4096,256]{1,0:T(8,128)}, f32[512,256]{1,0:T(8,128)}) custom-call(f32[4096,256]{1,0:T(8,128)} %modes.1, f32[32,4096]{1,0:T(8,128)} %bitcast.2, f32[32,4096]{1,0:T(8,128)} %bitcast.3, f32[256,256]{1,0:T(8,128)} %factor_one.1, f32[256,256]{1,0:T(8,128)} %factor_two.1), custom_call_target="tpu_custom_call" | custom-call | tf_op jit(solution)/shard_map/pallas_call | solution.py:331
  75.5 0.0 copy-start
  75.6 4.5 %copy.9 = f32[4096,256]{1,0:T(8,128)} copy(f32[4096,256]{1,0:T(8,128)} %get-tuple-element.4) | data formatting | bytes 8388608
  80.1 0.0 copy-done
  80.1 0.8 copy.10
Async XLA Ops:
  75.5 4.5 %copy-start = (f32[512,256]{1,0:T(8,128)S(1)}, f32[512,256]{1,0:T(8,128)}, u32[]{:S(2)}) copy-start(f32[512,256]{1,0:T(8,128)} %get-tuple-element.5) | copy-start | bytes 1572868

commit v2 on v1

v2 whole, which is shorter than its diff:
```python
import functools

import jax
import jax.numpy as jnp
from jax import lax
from jax.experimental import pallas as pl
from jax.experimental.pallas import tpu as pltpu
from jax.sharding import PartitionSpec as P

MESH = pl.DeviceIdType.MESH
F32, BF16 = jnp.float32, jnp.bfloat16
ROWS, COLS, NB = 4096, 256, 256
SHARE = 32
UNITS, UNIT = 4, 8
HALF = ROWS // 2
NX, NY, NZ = 4, 4, 8
GRAM = 10
STEP = 1024
PLACE = {0: 0, 1: 1, 3: 2, 2: 3}
AWAY = [0, 1, 3, 2]


def split(value):
    high = value.astype(BF16)
    return high, (value - high.astype(F32)).astype(BF16)


def dot(a, b):
    return jnp.dot(a, b, preferred_element_type=F32)


def exact(a, b):
    return jnp.dot(a, b, precision=lax.Precision.HIGHEST, preferred_element_type=F32)


def kernel(
    modes, panel_one, panel_two, factor_one, factor_two, work, coords,
    gathered, mode_high, mode_low, high, low, factors, part, from_x, from_z, sums, gram, right_side,
    load_sem, own_send, own_recv, fwd_send, fwd_recv, sib_send, sib_recv,
    x_send, x_recv, z_send, z_recv, back_send, back_recv, gram_send, gram_recv, gsib_send, gsib_recv,
):
    row, col = lax.axis_index("row"), lax.axis_index("col")
    z, x, y, k = row // NX, row % NX, col // 2, col % 2
    up, down = (row, lax.rem(y + 1, NY) * 2 + k), (row, lax.rem(y + NY - 1, NY) * 2 + k)
    sibling = (row, y * 2 + 1 - k)
    across = (row, lax.rem(y + 2, NY) * 2 + k)
    x_peer = [None] + [(z * NX + lax.rem(x + d, NX), col) for d in range(1, NX)]
    z_peer = [None] + [(lax.rem(z + d, NZ) * NX + x, col) for d in range(1, NZ)]
    panels = (panel_two, panel_one)
    mine = pl.ds(pl.multiple_of(k * SHARE, SHARE), SHARE)
    sends = []

    def remote(src, dst, send, recv, device):
        copy = pltpu.make_async_remote_copy(
            src_ref=src, dst_ref=dst, send_sem=send, recv_sem=recv, device_id=device, device_id_type=MESH
        )
        copy.start()
        sends.append(copy)
        return copy

    loads = []
    for p in range(2):
        loads.append(pltpu.make_async_copy(panels[p], gathered.at[p, mine], load_sem.at[p]))
    for i in range(8):
        rows = pl.ds(i * 512, 512)
        loads.append(pltpu.make_async_copy(modes.at[rows], work.at[rows], load_sem.at[4 + i]))
    loads.append(pltpu.make_async_copy(factor_two, factors.at[0], load_sem.at[2]))
    loads.append(pltpu.make_async_copy(factor_one, factors.at[1], load_sem.at[3]))
    for copy in loads:
        copy.start()

    barrier = pltpu.get_barrier_semaphore()
    friends = [up, down, across, sibling] + x_peer[1:] + z_peer[1:]
    for device in friends:
        pl.semaphore_signal(barrier, inc=1, device_id=device, device_id_type=MESH)
    pl.semaphore_wait(barrier, len(friends))

    def unit_rows(place, u):
        return pl.ds(pl.multiple_of(place * 64 + k * SHARE + u * UNIT, UNIT), UNIT)

    def send_own(p):
        got = {}
        for u in range(UNITS):
            src = panels[p].at[pl.ds(u * UNIT, UNIT)]
            for way, (device, away) in enumerate(((up, 3), (down, 1))):
                got[way, u] = remote(
                    src, gathered.at[p, unit_rows(PLACE[away], u)], own_send.at[p, way, u], own_recv.at[p, way, u], device
                )
        return got

    def to_sibling(p, place, u):
        rows = unit_rows(place, u)
        return remote(
            gathered.at[p, rows], gathered.at[p, rows], sib_send.at[p, place, u], sib_recv.at[p, place, u], sibling
        )

    def pass_on(p, own, u):
        copies = []
        for way, (device, away) in enumerate(((up, 3), (down, 1))):
            own[way, u].wait_recv()
            lanes = pl.ds(way * HALF, HALF)
            copies.append(remote(
                gathered.at[p, unit_rows(PLACE[away], u), lanes], gathered.at[p, unit_rows(3, u), lanes],
                fwd_send.at[p, way, u], fwd_recv.at[p, way, u], device,
            ))
        return copies, [to_sibling(p, PLACE[away], u) for away in (3, 1)]

    def multiply(p, slices, group):
        count = sum(n for _, n in slices)
        total = jnp.zeros((count, COLS), F32)
        for i in range(ROWS // STEP):
            lanes = slice(i * STEP, (i + 1) * STEP)
            rows = [gathered[p, at:at + n, lanes] for at, n in slices]
            h, l = split(rows[0] if len(rows) == 1 else jnp.concatenate(rows, axis=0))
            two = dot(jnp.concatenate([h, l], axis=0), mode_high[lanes])
            total += two[:count] + two[count:] + dot(h, mode_low[lanes])
        part[group, 0:count] = total

    def turn(p, pair):
        for i in range(ROWS // STEP):
            lanes = slice(i * STEP, (i + 1) * STEP)
            h, l = split(gathered[p, pair * 128:(pair + 1) * 128, lanes].T)
            high[p, lanes, pair * 128:(pair + 1) * 128] = h
            low[p, lanes, pair * 128:(pair + 1) * 128] = l

    class Group:
        def __init__(self, group, m, target, base):
            self.group, self.m, self.target, self.base = group, m, target, base

        def piece(self, at):
            return pl.ds(pl.multiple_of(at * self.m, self.m), self.m)

        def share_out(self):
            g, m = self.group, self.m
            self.copies = [
                remote(part.at[g, self.piece(lax.rem(x + d, NX))], from_x.at[g, d - 1, pl.ds(0, m)],
                       x_send.at[g, d - 1], x_recv.at[g, d - 1], x_peer[d])
                for d in range(1, NX)
            ]

        def to_z(self, value):
            g, m = self.group, self.m
            from_z[g, z, 0:m] = value
            self.copies = [
                remote(from_z.at[g, z, pl.ds(0, m)], from_z.at[g, z, pl.ds(0, m)],
                       z_send.at[g, d - 1], z_recv.at[g, d - 1], z_peer[d])
                for d in range(1, NZ)
            ]

        def exchange(self):
            g, m = self.group, self.m
            self.finish()
            self.to_z(part[g, self.piece(x)] + from_x[g, 0, 0:m] + from_x[g, 1, 0:m] + from_x[g, 2, 0:m])

        def z_sum(self):
            self.finish()
            total = from_z[self.group, 0, 0:self.m]
            for i in range(1, NZ):
                total += from_z[self.group, i, 0:self.m]
            return total

        def collect(self):
            g = self.group
            rows = pl.ds(pl.multiple_of(self.base, self.m), self.m)
            self.target[rows] = self.z_sum()
            self.copies = [
                remote(self.target.at[rows], self.target.at[rows], back_send.at[g, d - 1], back_recv.at[g, d - 1], x_peer[d])
                for d in range(1, NX)
            ]

        def finish(self):
            for copy in self.copies:
                copy.wait_recv()

    class Short(Group):
        def share_out(self):
            g = self.group
            from_x[g, x] = part[g, 0:16]
            self.copies = [
                remote(from_x.at[g, x], from_x.at[g, x], x_send.at[g, d - 1], x_recv.at[g, d - 1], x_peer[d])
                for d in range(1, NX)
            ]

        def exchange(self):
            g = self.group
            self.finish()
            self.to_z(((from_x[g, 0] + from_x[g, 1]) + from_x[g, 2]) + from_x[g, 3])

        def collect(self):
            total = self.z_sum()
            for core in range(2):
                self.target[pl.ds(pl.multiple_of(self.base + core * SHARE, UNIT), UNIT)] = total[core * UNIT:(core + 1) * UNIT]

    def block(away):
        return lax.rem(y + away, NY) * 64

    own = [Group(p, 16, sums.at[p], block(0) + x * 16) for p in range(2)]
    near = [
        [Group(2 + 2 * p + h, 16, sums.at[p], block(1 + 2 * (x // 2)) + (x % 2) * SHARE + h * 16) for h in range(2)]
        for p in range(2)
    ]
    far_two = Group(6, 16, sums.at[0], block(2) + x * 16)
    far_one = Group(7, 8, sums.at[1], block(2) + (x // 2) * SHARE + (x % 2) * UNIT)
    tail = [Short(8 + i, 16, sums.at[1], block(2) + (2 + i) * UNIT) for i in range(2)]
    gram_group = Group(GRAM, 8, gram, k * SHARE + x * 8)

    def near_rows(h):
        return [(place * 64 + core * SHARE + h * 16, 16) for place in (1, 2) for core in range(2)]

    def local(value, home):
        return jnp.concatenate(
            [value[pl.ds(pl.multiple_of(lax.rem(home + AWAY[s], NY) * 64, 64), 64)] for s in range(4)], axis=0
        )

    own_two = send_own(0)
    sib_own = []
    for p in range(2):
        for u in range(UNITS):
            rows = unit_rows(0, u)
            sib_own.append(remote(
                panels[p].at[pl.ds(u * UNIT, UNIT)], gathered.at[p, rows], sib_send.at[p, 0, u], sib_recv.at[p, 0, u], sibling
            ))
    for copy in loads:
        copy.wait()
    for i in range(8):
        rows = slice(i * 512, (i + 1) * 512)
        mode_high[rows], mode_low[rows] = split(work[rows])
    for copy in sib_own:
        copy.wait_recv()
    for p in range(2):
        multiply(p, [(0, 64)], p)
        own[p].share_out()

    def relay(p, sent, u):
        copies, swaps = pass_on(p, sent, u)
        return copies, swaps

    def wait(copies):
        for copy in copies:
            copy.wait_recv()

    def far_unit(p, copies, u):
        wait(copies)
        return to_sibling(p, 3, u)

    def gram_part():
        total = jnp.zeros((SHARE, NB), F32)
        for i in range(ROWS // STEP):
            lanes = slice(i * STEP, (i + 1) * STEP)
            h, l = split(gathered[1, mine, lanes])
            two = dot(jnp.concatenate([h, l], axis=0), high[0, lanes])
            total += two[:SHARE] + two[SHARE:] + dot(h, low[0, lanes])
        part[GRAM, 0:SHARE] = total

    def update(p, c, chunks):
        ch, cl = split(c)
        for i in chunks:
            rows = slice(i * 512, (i + 1) * 512)
            h = high[p, rows]
            work[rows] = work[rows] - (dot(h, ch) + dot(low[p, rows], ch) + dot(h, cl))

    on, swaps = [None] * UNITS, [None] * UNITS
    on[0], swaps[0] = relay(0, own_two, 0)
    own[0].exchange()
    own[1].exchange()
    on[1], swaps[1] = relay(0, own_two, 1)
    wait(swaps[0] + swaps[1])
    multiply(0, near_rows(0), near[0][0].group)
    near[0][0].share_out()
    on[2], swaps[2] = relay(0, own_two, 2)
    on[3], swaps[3] = relay(0, own_two, 3)
    own_one = send_own(1)
    near[0][0].exchange()
    wait(swaps[2] + swaps[3])
    multiply(0, near_rows(1), near[0][1].group)
    near[0][1].share_out()
    own[0].collect()
    own[1].collect()
    turn(0, 0)
    far = [far_unit(0, on[u], u) for u in range(UNITS)]
    near[0][1].exchange()
    wait(far)
    multiply(0, [(192, 64)], far_two.group)
    far_two.share_out()
    turn(0, 1)
    on[0], swaps[0] = relay(1, own_one, 0)
    gram_part()
    gram_group.share_out()
    near[0][0].collect()
    on[1], swaps[1] = relay(1, own_one, 1)
    far_two.exchange()
    wait(swaps[0] + swaps[1])
    multiply(1, near_rows(0), near[1][0].group)
    near[1][0].share_out()
    near[0][1].collect()
    on[2], swaps[2] = relay(1, own_one, 2)
    gram_group.exchange()
    on[3], swaps[3] = relay(1, own_one, 3)
    near[1][0].exchange()
    wait(swaps[2] + swaps[3])
    multiply(1, near_rows(1), near[1][1].group)
    near[1][1].share_out()
    far_two.collect()
    turn(1, 0)
    far = [far_unit(1, on[u], u) for u in range(2)]
    gram_group.collect()
    wait(far)
    multiply(1, [(192, 16), (224, 16)], far_one.group)
    far_one.share_out()
    far = [far_unit(1, on[2], 2)]
    for group in (own[0], near[0][0], near[0][1], far_two):
        group.finish()
    coords[NB:2 * NB] = exact(factors[0], sums[0])
    wait(far)
    multiply(1, [(208, 8), (240, 8)], tail[0].group)
    tail[0].share_out()
    near[1][1].exchange()
    far = [far_unit(1, on[3], 3)]
    wait(far)
    multiply(1, [(216, 8), (248, 8)], tail[1].group)
    tail[1].share_out()
    near[1][0].collect()
    far_one.exchange()
    gram_group.finish()
    around = [
        remote(gram.at[mine], gram.at[pl.ds(pl.multiple_of(away * 64 + k * SHARE, SHARE), SHARE)],
               gram_send.at[away], gram_recv.at[away], device)
        for away, device in ((3, up), (1, down), (2, across))
    ]
    two_at = coords.at[NB:2 * NB]
    near_two = local(two_at, y)
    tail[0].exchange()
    update(0, near_two, range(0, 3))
    tail[1].exchange()
    update(0, near_two, range(3, 8))
    near[1][1].collect()
    wait(around)
    swap = []
    for away in range(4):
        rows = pl.ds(pl.multiple_of(away * 64 + k * SHARE, SHARE), SHARE)
        swap.append(remote(gram.at[rows], gram.at[rows], gsib_send.at[away], gsib_recv.at[away], sibling))
    turn(1, 1)
    far_one.collect()
    wait(swap)
    for away in range(4):
        home = lax.rem(y + away, NY)
        right_side[pl.ds(pl.multiple_of(home * 64, 64), 64)] = exact(gram[away * 64:(away + 1) * 64], local(two_at, home))
    for group in (own[1], near[1][0], near[1][1], far_one):
        group.finish()
    tail[0].collect()
    tail[1].collect()
    coords[0:NB] = exact(factors[1], sums[1] - right_side[...])
    update(1, local(coords.at[0:NB], y), range(8))
    for copy in sends:
        copy.wait_send()


def shards(modes, panel_one, panel_two, factor_one, factor_two):
    hbm = pl.BlockSpec(memory_space=pltpu.HBM)
    dma = pltpu.SemaphoreType.DMA
    return pl.pallas_call(
        kernel,
        out_shape=(pltpu.VMEM((ROWS, COLS), F32), pltpu.VMEM((2 * NB, COLS), F32)),
        in_specs=[hbm] * 5,
        out_specs=(pl.BlockSpec(memory_space=pltpu.VMEM), pl.BlockSpec(memory_space=pltpu.VMEM)),
        scratch_shapes=[
            pltpu.VMEM((2, NB, ROWS), F32),
            pltpu.VMEM((ROWS, COLS), BF16),
            pltpu.VMEM((ROWS, COLS), BF16),
            pltpu.VMEM((2, ROWS, NB), BF16),
            pltpu.VMEM((2, ROWS, NB), BF16),
            pltpu.VMEM((2, NB, NB), F32),
            pltpu.VMEM((11, 64, COLS), F32),
            pltpu.VMEM((11, NX, 16, COLS), F32),
            pltpu.VMEM((11, NZ, 16, COLS), F32),
            pltpu.VMEM((2, NB, COLS), F32),
            pltpu.VMEM((NB, NB), F32),
            pltpu.VMEM((NB, COLS), F32),
            dma((12,)),
            dma((2, 2, UNITS)), dma((2, 2, UNITS)),
            dma((2, 2, UNITS)), dma((2, 2, UNITS)),
            dma((2, 4, UNITS)), dma((2, 4, UNITS)),
            dma((11, NX - 1)), dma((11, NX - 1)),
            dma((11, NZ - 1)), dma((11, NZ - 1)),
            dma((11, NX - 1)), dma((11, NX - 1)),
            dma((4,)), dma((4,)),
            dma((4,)), dma((4,)),
        ],
        compiler_params=pltpu.CompilerParams(collective_id=0, has_side_effects=True, vmem_limit_bytes=56 << 20),
    )(modes, panel_one.T, panel_two.T, factor_one, factor_two)


def solution(mesh):
    return jax.shard_map(
        shards,
        mesh=mesh,
        in_specs=(P("row", "col"), P("row", "col"), P("row", "col"), P(), P()),
        out_specs=(P("row", "col"), P(None, "col")),
        check_vma=False,
    )
```

time: 81 us -> 72.2 us (0.89)
  Pallas kernels: 74.9 us -> 68.6 us
  local copies, waits for them, and re-layouts: 5.33 us -> 2.81 us
    pallas_call x1, Pallas kernels: 74.9 us -> 68.6 us  [shards(): pl.pallas_call(kernel, out_shape=(pltpu.VMEM((ROWS, COLS), F32), pltpu.VM...]
    unnamed x4 -> x2, local copies, waits for them, and re-layouts: 5.33 us -> 2.81 us
where the time goes in v2:
time: 72.2 us; the launch traced here: 72.1 us
  Pallas kernels  68.6 us (95%)
  local copies, waits for them, and re-layouts  2.81 us (4%)
    pallas_call x1, Pallas kernels, shards(): pl.pallas_call(kernel, out_shape=(pltpu.VMEM((ROWS, COLS), F32), pltpu.VM...  68.6 us
    unnamed x2, local copies, waits for them, and re-layouts  2.81 us

profile of v2, /device:TPU:1, one launch (start us, length us, event | category | flops | bytes accessed | tf_op | source)
XLA Modules:
  0.0 72.1 jit_solution(7591028805367014164)
XLA Ops:
  0.6 68.6 %shard_map.68 = (f32[4096,256]{1,0:T(8,128)S(1)}, f32[512,256]{1,0:T(8,128)S(1)}) custom-call(f32[4096,256]{1,0:T(8,128)} %modes.1, f32[32,4096]{1,0:T(8,128)} %bitcast.2, f32[32,4096]{1,0:T(8,128)} %bitcast.3, f32[256,256]{1,0:T(8,128)} %factor_one.1, f32[256,256]{1,0:T(8,128)} %factor_two.1), custom_call_target="tpu_custom_call" | custom-call | tf_op jit(solution)/shard_map/pallas_call | solution.py:361
  69.3 2.0 %copy.9 = f32[4096,256]{1,0:T(8,128)} copy(f32[4096,256]{1,0:T(8,128)S(1)} %get-tuple-element.2) | data formatting | bytes 8388608
  71.3 0.8 %copy.10 = f32[512,256]{1,0:T(8,128)} copy(f32[512,256]{1,0:T(8,128)S(1)} %get-tuple-element.3) | data formatting | bytes 1048576

commit v3 on v2

--- a/solution.py
+++ b/solution.py
@@ -14,8 +14,8 @@
 UNITS, UNIT = 4, 8
 HALF = ROWS // 2
 NX, NY, NZ = 4, 4, 8
-GRAM = 10
-STEP = 1024
+GRAM = 12
+STEP, TURN = 2048, 512
 PLACE = {0: 0, 1: 1, 3: 2, 2: 3}
 AWAY = [0, 1, 3, 2]
 
@@ -29,13 +29,15 @@
     return jnp.dot(a, b, preferred_element_type=F32)
 
 
-def exact(a, b):
-    return jnp.dot(a, b, precision=lax.Precision.HIGHEST, preferred_element_type=F32)
+def triple(a, b):
+    ah, al = split(a)
+    bh, bl = split(b)
+    return dot(ah, bh) + (dot(al, bh) + dot(ah, bl))
 
 
 def kernel(
-    modes, panel_one, panel_two, factor_one, factor_two, work, coords,
-    gathered, mode_high, mode_low, high, low, factors, part, from_x, from_z, sums, gram, right_side,
+    modes, panel_one, panel_two, factor_one, factor_two, work, high_one, low_one, near_one, coords,
+    gathered, mode_high, mode_low, high_two, low_two, factors, part, from_x, from_z, sums, gram, right_side,
     load_sem, own_send, own_recv, fwd_send, fwd_recv, sib_send, sib_recv,
     x_send, x_recv, z_send, z_recv, back_send, back_recv, gram_send, gram_recv, gsib_send, gsib_recv,
 ):
@@ -47,6 +49,7 @@
     x_peer = [None] + [(z * NX + lax.rem(x + d, NX), col) for d in range(1, NX)]
     z_peer = [None] + [(lax.rem(z + d, NZ) * NX + x, col) for d in range(1, NZ)]
     panels = (panel_two, panel_one)
+    high, low = (high_two, high_one), (low_two, low_one)
     mine = pl.ds(pl.multiple_of(k * SHARE, SHARE), SHARE)
     sends = []
 
@@ -78,9 +81,8 @@
     def unit_rows(place, u):
         return pl.ds(pl.multiple_of(place * 64 + k * SHARE + u * UNIT, UNIT), UNIT)
 
-    def send_own(p):
-        got = {}
-        for u in range(UNITS):
+    def send_own(p, units, got):
+        for u in units:
             src = panels[p].at[pl.ds(u * UNIT, UNIT)]
             for way, (device, away) in enumerate(((up, 3), (down, 1))):
                 got[way, u] = remote(
@@ -107,21 +109,28 @@
 
     def multiply(p, slices, group):
         count = sum(n for _, n in slices)
-        total = jnp.zeros((count, COLS), F32)
-        for i in range(ROWS // STEP):
-            lanes = slice(i * STEP, (i + 1) * STEP)
+
+        def step(i, total):
+            lanes = pl.ds(pl.multiple_of(i * STEP, STEP), STEP)
             rows = [gathered[p, at:at + n, lanes] for at, n in slices]
             h, l = split(rows[0] if len(rows) == 1 else jnp.concatenate(rows, axis=0))
             two = dot(jnp.concatenate([h, l], axis=0), mode_high[lanes])
-            total += two[:count] + two[count:] + dot(h, mode_low[lanes])
-        part[group, 0:count] = total
+            return total + (two[:count] + two[count:] + dot(h, mode_low[lanes]))
+
+        total = lax.fori_loop(0, ROWS // STEP, step, jnp.zeros((count, COLS), F32))
+        if isinstance(group, tuple):
+            for i, g in enumerate(group):
+                part[g, 0:16] = total[i * 16:(i + 1) * 16]
+        else:
+            part[group, 0:count] = total
 
     def turn(p, pair):
-        for i in range(ROWS // STEP):
-            lanes = slice(i * STEP, (i + 1) * STEP)
+        @pl.loop(0, ROWS // TURN)
+        def _(i):
+            lanes = pl.ds(pl.multiple_of(i * TURN, TURN), TURN)
             h, l = split(gathered[p, pair * 128:(pair + 1) * 128, lanes].T)
-            high[p, lanes, pair * 128:(pair + 1) * 128] = h
-            low[p, lanes, pair * 128:(pair + 1) * 128] = l
+            high[p][lanes, pair * 128:(pair + 1) * 128] = h
+            low[p][lanes, pair * 128:(pair + 1) * 128] = l
 
     class Group:
         def __init__(self, group, m, target, base):
@@ -172,24 +181,41 @@
             for copy in self.copies:
                 copy.wait_recv()
 
-    class Short(Group):
+    class Ahead(Group):
         def share_out(self):
-            g = self.group
-            from_x[g, x] = part[g, 0:16]
+            self.to_x(part[self.group, 0:self.m])
+
+        def to_x(self, value):
+            g, m = self.group, self.m
+            from_x[g, x, 0:m] = value
             self.copies = [
-                remote(from_x.at[g, x], from_x.at[g, x], x_send.at[g, d - 1], x_recv.at[g, d - 1], x_peer[d])
+                remote(from_x.at[g, x, pl.ds(0, m)], from_x.at[g, x, pl.ds(0, m)], x_send.at[g, d - 1], x_recv.at[g, d - 1], x_peer[d])
                 for d in range(1, NX)
             ]
 
+        def x_sum(self):
+            self.finish()
+            g, m = self.group, self.m
+            return ((from_x[g, 0, 0:m] + from_x[g, 1, 0:m]) + from_x[g, 2, 0:m]) + from_x[g, 3, 0:m]
+
         def exchange(self):
-            g = self.group
-            self.finish()
-            self.to_z(((from_x[g, 0] + from_x[g, 1]) + from_x[g, 2]) + from_x[g, 3])
+            self.to_z(self.x_sum())
 
         def collect(self):
-            total = self.z_sum()
-            for core in range(2):
-                self.target[pl.ds(pl.multiple_of(self.base + core * SHARE, UNIT), UNIT)] = total[core * UNIT:(core + 1) * UNIT]
+            self.store(self.z_sum())
+
+        def store(self, total):
+            self.target[pl.ds(pl.multiple_of(self.base, self.m), self.m)] = total
+
+    class Behind(Ahead):
+        def share_out(self):
+            self.to_z(part[self.group, 0:self.m])
+
+        def exchange(self):
+            self.to_x(self.z_sum())
+
+        def collect(self):
+            self.store(self.x_sum())
 
     def block(away):
         return lax.rem(y + away, NY) * 64
@@ -201,7 +227,7 @@
     ]
     far_two = Group(6, 16, sums.at[0], block(2) + x * 16)
     far_one = Group(7, 8, sums.at[1], block(2) + (x // 2) * SHARE + (x % 2) * UNIT)
-    tail = [Short(8 + i, 16, sums.at[1], block(2) + (2 + i) * UNIT) for i in range(2)]
+    tail = [kind(8 + core, 16, sums.at[1], block(2) + core * SHARE + 16) for core, kind in enumerate((Ahead, Behind))]
     gram_group = Group(GRAM, 8, gram, k * SHARE + x * 8)
 
     def near_rows(h):
@@ -212,7 +238,7 @@
             [value[pl.ds(pl.multiple_of(lax.rem(home + AWAY[s], NY) * 64, 64), 64)] for s in range(4)], axis=0
         )
 
-    own_two = send_own(0)
+    own_two = send_own(0, range(UNITS), {})
     sib_own = []
     for p in range(2):
         for u in range(UNITS):
@@ -222,9 +248,12 @@
             ))
     for copy in loads:
         copy.wait()
-    for i in range(8):
-        rows = slice(i * 512, (i + 1) * 512)
+
+    @pl.loop(0, 8)
+    def _(i):
+        rows = pl.ds(pl.multiple_of(i * 512, 512), 512)
         mode_high[rows], mode_low[rows] = split(work[rows])
+
     for copy in sib_own:
         copy.wait_recv()
     for p in range(2):
@@ -244,20 +273,21 @@
         return to_sibling(p, 3, u)
 
     def gram_part():
-        total = jnp.zeros((SHARE, NB), F32)
-        for i in range(ROWS // STEP):
-            lanes = slice(i * STEP, (i + 1) * STEP)
+        def step(i, total):
+            lanes = pl.ds(pl.multiple_of(i * STEP, STEP), STEP)
             h, l = split(gathered[1, mine, lanes])
-            two = dot(jnp.concatenate([h, l], axis=0), high[0, lanes])
-            total += two[:SHARE] + two[SHARE:] + dot(h, low[0, lanes])
-        part[GRAM, 0:SHARE] = total
+            two = dot(jnp.concatenate([h, l], axis=0), high_two[lanes])
+            return total + (two[:SHARE] + two[SHARE:] + dot(h, low_two[lanes]))
+
+        part[GRAM, 0:SHARE] = lax.fori_loop(0, ROWS // STEP, step, jnp.zeros((SHARE, NB), F32))
 
     def update(p, c, chunks):
         ch, cl = split(c)
-        for i in chunks:
-            rows = slice(i * 512, (i + 1) * 512)
-            h = high[p, rows]
-            work[rows] = work[rows] - (dot(h, ch) + dot(low[p, rows], ch) + dot(h, cl))
+        @pl.loop(chunks.start, chunks.stop)
+        def _(i):
+            rows = pl.ds(pl.multiple_of(i * 512, 512), 512)
+            h = high[p][rows]
+            work[rows] = work[rows] - (dot(h, ch) + dot(low[p][rows], ch) + dot(h, cl))
 
     on, swaps = [None] * UNITS, [None] * UNITS
     on[0], swaps[0] = relay(0, own_two, 0)
@@ -269,7 +299,7 @@
     near[0][0].share_out()
     on[2], swaps[2] = relay(0, own_two, 2)
     on[3], swaps[3] = relay(0, own_two, 3)
-    own_one = send_own(1)
+    own_one = send_own(1, range(UNITS), {})
     near[0][0].exchange()
     wait(swaps[2] + swaps[3])
     multiply(0, near_rows(1), near[0][1].group)
@@ -300,25 +330,19 @@
     wait(swaps[2] + swaps[3])
     multiply(1, near_rows(1), near[1][1].group)
     near[1][1].share_out()
+    far = [far_unit(1, on[u], u) for u in range(2)]
     far_two.collect()
-    turn(1, 0)
-    far = [far_unit(1, on[u], u) for u in range(2)]
     gram_group.collect()
     wait(far)
     multiply(1, [(192, 16), (224, 16)], far_one.group)
     far_one.share_out()
     far = [far_unit(1, on[2], 2)]
-    for group in (own[0], near[0][0], near[0][1], far_two):
-        group.finish()
-    coords[NB:2 * NB] = exact(factors[0], sums[0])
+    near[1][1].exchange()
+    far.append(far_unit(1, on[3], 3))
     wait(far)
-    multiply(1, [(208, 8), (240, 8)], tail[0].group)
+    multiply(1, [(208, 16), (240, 16)], (8, 9))
+    tail[1].share_out()
     tail[0].share_out()
-    near[1][1].exchange()
-    far = [far_unit(1, on[3], 3)]
-    wait(far)
-    multiply(1, [(216, 8), (248, 8)], tail[1].group)
-    tail[1].share_out()
     near[1][0].collect()
     far_one.exchange()
     gram_group.finish()
@@ -327,52 +351,77 @@
                gram_send.at[away], gram_recv.at[away], device)
         for away, device in ((3, up), (1, down), (2, across))
     ]
+    for group in (own[0], near[0][0], near[0][1], far_two):
+        group.finish()
+    coords[NB:2 * NB] = triple(factors[0], sums[0])
     two_at = coords.at[NB:2 * NB]
     near_two = local(two_at, y)
+    turn(1, 0)
     tail[0].exchange()
     update(0, near_two, range(0, 3))
-    tail[1].exchange()
-    update(0, near_two, range(3, 8))
     near[1][1].collect()
     wait(around)
     swap = []
     for away in range(4):
         rows = pl.ds(pl.multiple_of(away * 64 + k * SHARE, SHARE), SHARE)
         swap.append(remote(gram.at[rows], gram.at[rows], gsib_send.at[away], gsib_recv.at[away], sibling))
+    tail[1].exchange()
+    far_one.collect()
+    update(0, near_two, range(3, 8))
     turn(1, 1)
-    far_one.collect()
     wait(swap)
     for away in range(4):
         home = lax.rem(y + away, NY)
-        right_side[pl.ds(pl.multiple_of(home * 64, 64), 64)] = exact(gram[away * 64:(away + 1) * 64], local(two_at, home))
+        right_side[pl.ds(pl.multiple_of(home * 64, 64), 64)] = triple(gram[away * 64:(away + 1) * 64], local(two_at, home))
     for group in (own[1], near[1][0], near[1][1], far_one):
         group.finish()
-    tail[0].collect()
-    tail[1].collect()
-    coords[0:NB] = exact(factors[1], sums[1] - right_side[...])
-    update(1, local(coords.at[0:NB], y), range(8))
+    for group in tail:
+        group.collect()
+    coords[0:NB] = triple(factors[1], sums[1] - right_side[...])
+    near_one[...] = local(coords.at[0:NB], y)
     for copy in sends:
         copy.wait_send()
 
 
+CHUNKS = 8
+
+
+def last_update(work, high, low, near_one, coords, updated, coords_out, stage, sem):
+    copies = [pltpu.make_async_copy(coords, coords_out, sem.at[CHUNKS])]
+    copies[0].start()
+    ch, cl = split(near_one[...])
+    size = ROWS // CHUNKS
+    for i in range(CHUNKS):
+        rows = slice(i * size, (i + 1) * size)
+        h = high[rows]
+        stage[rows] = work[rows] - (dot(h, ch) + dot(low[rows], ch) + dot(h, cl))
+        copies.append(pltpu.make_async_copy(stage.at[rows], updated.at[rows], sem.at[i]))
+        copies[-1].start()
+    for copy in copies:
+        copy.wait()
+
+
 def shards(modes, panel_one, panel_two, factor_one, factor_two):
-    hbm = pl.BlockSpec(memory_space=pltpu.HBM)
+    hbm, vmem = pl.BlockSpec(memory_space=pltpu.HBM), pl.BlockSpec(memory_space=pltpu.VMEM)
     dma = pltpu.SemaphoreType.DMA
-    return pl.pallas_call(
+    state = pl.pallas_call(
         kernel,
-        out_shape=(pltpu.VMEM((ROWS, COLS), F32), pltpu.VMEM((2 * NB, COLS), F32)),
+        out_shape=(
+            pltpu.VMEM((ROWS, COLS), F32), pltpu.VMEM((ROWS, NB), BF16), pltpu.VMEM((ROWS, NB), BF16),
+            pltpu.VMEM((NB, COLS), F32), pltpu.VMEM((2 * NB, COLS), F32),
+        ),
         in_specs=[hbm] * 5,
-        out_specs=(pl.BlockSpec(memory_space=pltpu.VMEM), pl.BlockSpec(memory_space=pltpu.VMEM)),
+        out_specs=(vmem,) * 5,
         scratch_shapes=[
             pltpu.VMEM((2, NB, ROWS), F32),
             pltpu.VMEM((ROWS, COLS), BF16),
             pltpu.VMEM((ROWS, COLS), BF16),
-            pltpu.VMEM((2, ROWS, NB), BF16),
-            pltpu.VMEM((2, ROWS, NB), BF16),
+            pltpu.VMEM((ROWS, NB), BF16),
+            pltpu.VMEM((ROWS, NB), BF16),
             pltpu.VMEM((2, NB, NB), F32),
-            pltpu.VMEM((11, 64, COLS), F32),
-            pltpu.VMEM((11, NX, 16, COLS), F32),
-            pltpu.VMEM((11, NZ, 16, COLS), F32),
+            pltpu.VMEM((13, 64, COLS), F32),
+            pltpu.VMEM((13, NX, 16, COLS), F32),
+            pltpu.VMEM((13, NZ, 16, COLS), F32),
             pltpu.VMEM((2, NB, COLS), F32),
             pltpu.VMEM((NB, NB), F32),
             pltpu.VMEM((NB, COLS), F32),
@@ -380,14 +429,22 @@
             dma((2, 2, UNITS)), dma((2, 2, UNITS)),
             dma((2, 2, UNITS)), dma((2, 2, UNITS)),
             dma((2, 4, UNITS)), dma((2, 4, UNITS)),
-            dma((11, NX - 1)), dma((11, NX - 1)),
-            dma((11, NZ - 1)), dma((11, NZ - 1)),
-            dma((11, NX - 1)), dma((11, NX - 1)),
+            dma((13, NX - 1)), dma((13, NX - 1)),
+            dma((13, NZ - 1)), dma((13, NZ - 1)),
+            dma((13, NX - 1)), dma((13, NX - 1)),
             dma((4,)), dma((4,)),
             dma((4,)), dma((4,)),
         ],
-        compiler_params=pltpu.CompilerParams(collective_id=0, has_side_effects=True, vmem_limit_bytes=56 << 20),
+        compiler_params=pltpu.CompilerParams(collective_id=0, has_side_effects=True, vmem_limit_bytes=54 << 20),
     )(modes, panel_one.T, panel_two.T, factor_one, factor_two)
+    return pl.pallas_call(
+        last_update,
+        out_shape=(jax.ShapeDtypeStruct((ROWS, COLS), F32), jax.ShapeDtypeStruct((2 * NB, COLS), F32)),
+        in_specs=[vmem] * 5,
+        out_specs=(hbm, hbm),
+        scratch_shapes=[pltpu.VMEM((ROWS, COLS), F32), dma((CHUNKS + 1,))],
+        compiler_params=pltpu.CompilerParams(vmem_limit_bytes=24 << 20),
+    )(*state)
 
 
 def solution(mesh):

time: 72.2 us -> 69.2 us (0.958)
  local copies, waits for them, and re-layouts: 2.81 us -> 0 us
    pallas_call x1, Pallas kernels: 68.6 us -> 65.4 us  [shards(): pl.pallas_call(kernel, out_shape=(pltpu.VMEM((ROWS, COLS), F32), pltpu.VM...]
    pallas_call x0 -> x1, Pallas kernels: none -> 3.07 us  [shards(): pl.pallas_call(last_update, out_shape=(jax.ShapeDtypeStruct((ROWS, COLS),...]
    unnamed x2 -> x0, local copies, waits for them, and re-layouts: 2.81 us -> none
where the time goes in v3:
time: 69.2 us; the launch traced here: 69.1 us
  Pallas kernels  68.5 us (99%)
    pallas_call x1, Pallas kernels, shards(): pl.pallas_call(kernel, out_shape=(pltpu.VMEM((ROWS, COLS), F32), pltpu.VM...  65.4 us
    pallas_call x1, Pallas kernels, shards(): pl.pallas_call(last_update, out_shape=(jax.ShapeDtypeStruct((ROWS, COLS),...  3.07 us

profile of v3, /device:TPU:1, one launch (start us, length us, event | category | flops | bytes accessed | tf_op | source)
XLA Modules:
  0.0 69.1 jit_solution(2835771082451458522)
XLA Ops:
  0.6 65.4 %shard_map.68 = (f32[4096,256]{1,0:T(8,128)S(1)}, bf16[4096,256]{1,0:T(8,128)(2,1)S(1)}, bf16[4096,256]{1,0:T(8,128)(2,1)S(1)}, f32[256,256]{1,0:T(8,128)S(1)}, f32[512,256]{1,0:T(8,128)S(1)}) custom-call(f32[4096,256]{1,0:T(8,128)} %modes.1, f32[32,4096]{1,0:T(8,128)} %bitcast.2, f32[32,4096]{1,0:T(8,128)} %bitcast.3, f32[256,256]{1,0:T(8,128)} %factor_one.1, ...), custom_call_target="tpu_custom_call" | custom-call | tf_op jit(solution)/shard_map/pallas_call | solution.py:407
  66.1 3.1 %shard_map.69 = (f32[4096,256]{1,0:T(8,128)}, f32[512,256]{1,0:T(8,128)}) custom-call(f32[4096,256]{1,0:T(8,128)S(1)} %get-tuple-element.7.work, bf16[4096,256]{1,0:T(8,128)(2,1)S(1)} %get-tuple-element.8.high, bf16[4096,256]{1,0:T(8,128)(2,1)S(1)} %get-tuple-element.9.low, f32[256,256]{1,0:T(8,128)S(1)} %get-tuple-element.10.near_one, ...), custom_call_target="tpu_custom_call" | custom-call | tf_op jit(solution)/shard_map/pallas_call | solution.py:440

commit v4 on v3

--- a/solution.py
+++ b/solution.py
@@ -118,11 +118,7 @@
             return total + (two[:count] + two[count:] + dot(h, mode_low[lanes]))
 
         total = lax.fori_loop(0, ROWS // STEP, step, jnp.zeros((count, COLS), F32))
-        if isinstance(group, tuple):
-            for i, g in enumerate(group):
-                part[g, 0:16] = total[i * 16:(i + 1) * 16]
-        else:
-            part[group, 0:count] = total
+        part[group, 0:count] = total
 
     def turn(p, pair):
         @pl.loop(0, ROWS // TURN)
@@ -181,42 +177,6 @@
             for copy in self.copies:
                 copy.wait_recv()
 
-    class Ahead(Group):
-        def share_out(self):
-            self.to_x(part[self.group, 0:self.m])
-
-        def to_x(self, value):
-            g, m = self.group, self.m
-            from_x[g, x, 0:m] = value
-            self.copies = [
-                remote(from_x.at[g, x, pl.ds(0, m)], from_x.at[g, x, pl.ds(0, m)], x_send.at[g, d - 1], x_recv.at[g, d - 1], x_peer[d])
-                for d in range(1, NX)
-            ]
-
-        def x_sum(self):
-            self.finish()
-            g, m = self.group, self.m
-            return ((from_x[g, 0, 0:m] + from_x[g, 1, 0:m]) + from_x[g, 2, 0:m]) + from_x[g, 3, 0:m]
-
-        def exchange(self):
-            self.to_z(self.x_sum())
-
-        def collect(self):
-            self.store(self.z_sum())
-
-        def store(self, total):
-            self.target[pl.ds(pl.multiple_of(self.base, self.m), self.m)] = total
-
-    class Behind(Ahead):
-        def share_out(self):
-            self.to_z(part[self.group, 0:self.m])
-
-        def exchange(self):
-            self.to_x(self.z_sum())
-
-        def collect(self):
-            self.store(self.x_sum())
-
     def block(away):
         return lax.rem(y + away, NY) * 64
 
@@ -227,7 +187,7 @@
     ]
     far_two = Group(6, 16, sums.at[0], block(2) + x * 16)
     far_one = Group(7, 8, sums.at[1], block(2) + (x // 2) * SHARE + (x % 2) * UNIT)
-    tail = [kind(8 + core, 16, sums.at[1], block(2) + core * SHARE + 16) for core, kind in enumerate((Ahead, Behind))]
+    tail = Group(8, 8, sums.at[1], block(2) + (x // 2) * SHARE + 16 + (x % 2) * UNIT)
     gram_group = Group(GRAM, 8, gram, k * SHARE + x * 8)
 
     def near_rows(h):
@@ -330,8 +290,8 @@
     wait(swaps[2] + swaps[3])
     multiply(1, near_rows(1), near[1][1].group)
     near[1][1].share_out()
+    far_two.collect()
     far = [far_unit(1, on[u], u) for u in range(2)]
-    far_two.collect()
     gram_group.collect()
     wait(far)
     multiply(1, [(192, 16), (224, 16)], far_one.group)
@@ -339,10 +299,12 @@
     far = [far_unit(1, on[2], 2)]
     near[1][1].exchange()
     far.append(far_unit(1, on[3], 3))
+    for group in (own[0], near[0][0], near[0][1], far_two):
+        group.finish()
+    coords[NB:2 * NB] = triple(factors[0], sums[0])
     wait(far)
-    multiply(1, [(208, 16), (240, 16)], (8, 9))
-    tail[1].share_out()
-    tail[0].share_out()
+    multiply(1, [(208, 16), (240, 16)], 8)
+    tail.share_out()
     near[1][0].collect()
     far_one.exchange()
     gram_group.finish()
@@ -351,13 +313,10 @@
                gram_send.at[away], gram_recv.at[away], device)
         for away, device in ((3, up), (1, down), (2, across))
     ]
-    for group in (own[0], near[0][0], near[0][1], far_two):
-        group.finish()
-    coords[NB:2 * NB] = triple(factors[0], sums[0])
     two_at = coords.at[NB:2 * NB]
     near_two = local(two_at, y)
     turn(1, 0)
-    tail[0].exchange()
+    tail.exchange()
     update(0, near_two, range(0, 3))
     near[1][1].collect()
     wait(around)
@@ -365,18 +324,16 @@
     for away in range(4):
         rows = pl.ds(pl.multiple_of(away * 64 + k * SHARE, SHARE), SHARE)
         swap.append(remote(gram.at[rows], gram.at[rows], gsib_send.at[away], gsib_recv.at[away], sibling))
-    tail[1].exchange()
     far_one.collect()
     update(0, near_two, range(3, 8))
-    turn(1, 1)
     wait(swap)
     for away in range(4):
         home = lax.rem(y + away, NY)
         right_side[pl.ds(pl.multiple_of(home * 64, 64), 64)] = triple(gram[away * 64:(away + 1) * 64], local(two_at, home))
-    for group in (own[1], near[1][0], near[1][1], far_one):
+    tail.collect()
+    turn(1, 1)
+    for group in (own[1], near[1][0], near[1][1], far_one, tail):
         group.finish()
-    for group in tail:
-        group.collect()
     coords[0:NB] = triple(factors[1], sums[1] - right_side[...])
     near_one[...] = local(coords.at[0:NB], y)
     for copy in sends:

time: 69.2 us -> 67.8 us (0.980)
  Pallas kernels: 68.5 us -> 67.1 us
    pallas_call x1, Pallas kernels: 65.4 us -> 64 us  [shards(): pl.pallas_call(kernel, out_shape=(pltpu.VMEM((ROWS, COLS), F32), pltpu.VM...]
where the time goes in v4:
time: 67.8 us; the launch traced here: 67.7 us
  Pallas kernels  67.1 us (99%)
    pallas_call x1, Pallas kernels, shards(): pl.pallas_call(kernel, out_shape=(pltpu.VMEM((ROWS, COLS), F32), pltpu.VM...  64 us
    pallas_call x1, Pallas kernels, shards(): pl.pallas_call(last_update, out_shape=(jax.ShapeDtypeStruct((ROWS, COLS),...  3.07 us

profile of v4, /device:TPU:1, one launch (start us, length us, event | category | flops | bytes accessed | tf_op | source)
XLA Modules:
  0.0 67.7 jit_solution(8029990084683761636)
XLA Ops:
  0.6 64.0 %shard_map.68 = (f32[4096,256]{1,0:T(8,128)S(1)}, bf16[4096,256]{1,0:T(8,128)(2,1)S(1)}, bf16[4096,256]{1,0:T(8,128)(2,1)S(1)}, f32[256,256]{1,0:T(8,128)S(1)}, f32[512,256]{1,0:T(8,128)S(1)}) custom-call(f32[4096,256]{1,0:T(8,128)} %modes.1, f32[32,4096]{1,0:T(8,128)} %bitcast.2, f32[32,4096]{1,0:T(8,128)} %bitcast.3, f32[256,256]{1,0:T(8,128)} %factor_one.1, ...), custom_call_target="tpu_custom_call" | custom-call | tf_op jit(solution)/shard_map/pallas_call | solution.py:364
  64.7 3.1 %shard_map.69 = (f32[4096,256]{1,0:T(8,128)}, f32[512,256]{1,0:T(8,128)}) custom-call(f32[4096,256]{1,0:T(8,128)S(1)} %get-tuple-element.7.work, bf16[4096,256]{1,0:T(8,128)(2,1)S(1)} %get-tuple-element.8.high, bf16[4096,256]{1,0:T(8,128)(2,1)S(1)} %get-tuple-element.9.low, f32[256,256]{1,0:T(8,128)S(1)} %get-tuple-element.10.near_one, ...), custom_call_target="tpu_custom_call" | custom-call | tf_op jit(solution)/shard_map/pallas_call | solution.py:397

commit v5 on v4

--- a/solution.py
+++ b/solution.py
@@ -296,8 +296,8 @@
     wait(far)
     multiply(1, [(192, 16), (224, 16)], far_one.group)
     far_one.share_out()
+    near[1][1].exchange()
     far = [far_unit(1, on[2], 2)]
-    near[1][1].exchange()
     far.append(far_unit(1, on[3], 3))
     for group in (own[0], near[0][0], near[0][1], far_two):
         group.finish()

time: 67.8 us -> 67.9 us (level)
  no operation moved by 1% of the time
where the time goes in v5:
time: 67.9 us; the launch traced here: 67.7 us
  Pallas kernels  67.1 us (99%)
    pallas_call x1, Pallas kernels, shards(): pl.pallas_call(kernel, out_shape=(pltpu.VMEM((ROWS, COLS), F32), pltpu.VM...  64 us
    pallas_call x1, Pallas kernels, shards(): pl.pallas_call(last_update, out_shape=(jax.ShapeDtypeStruct((ROWS, COLS),...  3.06 us

profile of v5, /device:TPU:1, one launch (start us, length us, event | category | flops | bytes accessed | tf_op | source)
XLA Modules:
  0.0 67.7 jit_solution(16286353074633094898)
XLA Ops:
  0.6 64.0 %shard_map.68 = (f32[4096,256]{1,0:T(8,128)S(1)}, bf16[4096,256]{1,0:T(8,128)(2,1)S(1)}, bf16[4096,256]{1,0:T(8,128)(2,1)S(1)}, f32[256,256]{1,0:T(8,128)S(1)}, f32[512,256]{1,0:T(8,128)S(1)}) custom-call(f32[4096,256]{1,0:T(8,128)} %modes.1, f32[32,4096]{1,0:T(8,128)} %bitcast.2, f32[32,4096]{1,0:T(8,128)} %bitcast.3, f32[256,256]{1,0:T(8,128)} %factor_one.1, ...), custom_call_target="tpu_custom_call" | custom-call | tf_op jit(solution)/shard_map/pallas_call | solution.py:364
  64.6 3.1 %shard_map.69 = (f32[4096,256]{1,0:T(8,128)}, f32[512,256]{1,0:T(8,128)}) custom-call(f32[4096,256]{1,0:T(8,128)S(1)} %get-tuple-element.7.work, bf16[4096,256]{1,0:T(8,128)(2,1)S(1)} %get-tuple-element.8.high, bf16[4096,256]{1,0:T(8,128)(2,1)S(1)} %get-tuple-element.9.low, f32[256,256]{1,0:T(8,128)S(1)} %get-tuple-element.10.near_one, ...), custom_call_target="tpu_custom_call" | custom-call | tf_op jit(solution)/shard_map/pallas_call | solution.py:397
